TPU v7x, 256 devices: a whole 4x4x8 slice. The times are simulated.
256 devices in a mesh: ctx: 32 (over x, z), head: 8 (over y, core).
Axes of the slice: x: 4, y: 4, z: 8, core: 2. Of those that a mesh axis runs over, the one named last changes fastest.
Arguments:
- ssm_input: bfloat16 [8192, 8192], P('ctx', 'head'), may hold values from -6 to 6
- gate_input: bfloat16 [8192, 8192], P('ctx', 'head'), may hold values from -6 to 6
- in_state: bfloat16 [8192, 1024], P('ctx', 'head'), may hold values from -0.5 to 0.5
- out_state: bfloat16 [8192, 1024], P('ctx', 'head'), may hold values from -0.5 to 0.5
- step_size: float32 [8192, 128], P('ctx', 'head'), may hold values from 0.05 to 0.5
- log_decay: float32 [8192, 128], P('ctx', 'head'), may hold values from 0 to 2
- skip_gain: float32 [128], P('head'), may hold values from 0.5 to 1.5
- norm_gain: float32 [8192], P('head'), may hold values from 0.5 to 1.5
- queries: bfloat16 [8192, 8192], P('ctx', 'head'), may hold values from -5 to 5
- keys: bfloat16 [8192, 1024], P('ctx', 'head'), may hold values from -5 to 5
- values: bfloat16 [8192, 1024], P('ctx', 'head'), may hold values from -6 to 6
Outputs:
- mamba_out: bfloat16 [8192, 8192], P('ctx', 'head')
- attention_out: bfloat16 [8192, 8192], P('ctx', 'head')
All inputs are finite; a program needn't handle non-finite values.
Results may differ from a plain program's by a relative error of at most 0.014.
Values may be sent and summed in bfloat16 or wider, within the bound.
No kernel may reach another device: no remote copies, remote signals or barrier semaphores. Data moves between devices by JAX's collectives and lax.ppermute only.
A program may use at most 128 MiB of HBM per device.

v0:
```python
import jax
import jax.numpy as jnp
from jax import lax
from jax.sharding import PartitionSpec as P

MIXER_HEADS = 128
P_SIZE = 64
N = 128
HQ = 64
KVH = 8
DH = 128
BLOCK = 256
HIGH = lax.Precision.HIGHEST


def carried_in(value, axis, join, neutral):
    place = lax.axis_index(axis)
    gathered = jax.tree.map(
        lambda a, kind: lax.all_gather(a.astype(kind), axis), value, (jnp.bfloat16, jnp.bfloat16)
    )
    state = jax.tree.map(lambda a, e: jnp.zeros_like(a) + jnp.asarray(e, a.dtype), value, neutral)

    def one(turn, state):
        return join(
            state,
            jax.tree.map(
                lambda a, own: lax.dynamic_index_in_dim(a, turn, 0, False).astype(own.dtype),
                gathered,
                value,
            ),
        )

    return lax.fori_loop(0, place, one, state)


def block_segments(signal, enter, enter_half, leave_half, step_size, decay):
    length = signal.shape[0]
    running_state = jnp.cumsum(decay, axis=0)
    scaled = signal * step_size[..., None]
    affinity = jnp.einsum(
        "tgn,sgn->tsg", leave_half, enter_half, preferred_element_type=jnp.float32
    )
    order = jnp.arange(length, dtype=jnp.int32)
    causal = (order[:, None] >= order[None, :])[:, :, None, None]
    spread = jnp.where(causal, running_state[:, None] - running_state[None, :], 0.0)
    mixing = jnp.where(causal, jnp.exp(-spread), 0.0) * affinity[..., None]
    within_block = jnp.einsum("tsgk,sgkp->tgkp", mixing, scaled, precision=HIGH)
    total_sum = running_state[-1]
    remain = jnp.exp(running_state - total_sum[None])
    state_contribution = jnp.einsum(
        "sgn,sgkp->gknp", enter, scaled * remain[..., None], precision=HIGH
    )
    return (within_block, state_contribution, jnp.exp(-total_sum), running_state, total_sum)


def past_carryover(leave, running_state, state_matrix):
    return (
        jnp.einsum("tgn,gknp->tgkp", leave, state_matrix, precision=HIGH)
        * jnp.exp(-running_state)[..., None]
    )


def mamba_mixer(
    ssm_input, gate_input, in_state, out_state, step_size, log_decay, skip_gain, norm_gain
):
    tokens_here = ssm_input.shape[0]
    count = tokens_here // BLOCK
    heads_here = skip_gain.shape[0]
    groups_here = in_state.shape[1] // N
    per_group = heads_here // groups_here
    signal = ssm_input.astype(jnp.float32).reshape(count, BLOCK, groups_here, per_group, P_SIZE)
    enter_half = in_state.reshape(count, BLOCK, groups_here, N)
    leave_half = out_state.reshape(count, BLOCK, groups_here, N)
    enter = enter_half.astype(jnp.float32)
    leave = leave_half.astype(jnp.float32)
    stepped = step_size.reshape(count, BLOCK, groups_here, per_group)
    decay = log_decay.reshape(count, BLOCK, groups_here, per_group)
    skip_path = skip_gain.reshape(groups_here, per_group)
    pieces = block_segments(signal[0], enter[0], enter_half[0], leave_half[0], stepped[0], decay[0])
    fade_all = jnp.ones((groups_here, per_group), jnp.float32)
    carried = jnp.zeros((groups_here, per_group, N, P_SIZE), jnp.float32)
    carried = pieces[2][..., None, None] * carried + pieces[1]
    fade_all = fade_all * pieces[2]

    def combine(earlier, later):
        return (earlier[0] * later[0], later[0][..., None, None] * earlier[1] + later[1])

    identity = (jnp.ones_like(fade_all), jnp.zeros_like(carried))
    _, state_matrix = carried_in((fade_all, carried), "ctx", combine, identity)
    within_block, state_contribution, fading_factor, running_state, total_sum = pieces
    mixed_output = (
        within_block
        + past_carryover(leave[0], running_state, state_matrix)
        + skip_path[..., None] * signal[0]
    )
    outputs = [mixed_output]
    mixed_output = jnp.stack(outputs).reshape(tokens_here, heads_here * P_SIZE)
    gated = mixed_output * jax.nn.silu(gate_input.astype(jnp.float32))
    squares = lax.psum(jnp.sum(gated * gated, axis=1), "head")
    scale = lax.rsqrt(squares / (MIXER_HEADS * P_SIZE) + 1e-05)
    return (gated * scale[:, None] * norm_gain).astype(jnp.bfloat16)


def attention(queries, keys, values):
    tokens_here = queries.shape[0]
    kv_here = keys.shape[1] // DH
    per_kv = HQ // KVH
    query_rows = queries.reshape(tokens_here, kv_here, per_kv, DH)
    first = lax.axis_index("ctx") * tokens_here
    query_pos = first + jnp.arange(tokens_here, dtype=jnp.int32)
    factor = DH ** (-0.5)

    def update(carry, key_block, value_block, key_pos):
        peak, total_sum, summed = carry
        score = (
            jnp.einsum("tgqd,jgd->gqtj", query_rows, key_block, preferred_element_type=jnp.float32)
            * factor
        )
        mask = (key_pos[None, :] <= query_pos[:, None])[None, None]
        block_peak = jnp.max(jnp.where(mask, score, -1e30), axis=-1)
        new_peak = jnp.maximum(peak, block_peak)
        weight = jnp.where(mask, jnp.exp(score - new_peak[..., None]), 0.0)
        shrink = jnp.exp(peak - new_peak)
        total_sum = total_sum * shrink + jnp.sum(weight, axis=-1)
        summed = summed * shrink[..., None] + jnp.einsum(
            "gqtj,jgd->gqtd",
            weight.astype(jnp.bfloat16),
            value_block,
            preferred_element_type=jnp.float32,
        )
        return (new_peak, total_sum, summed)

    initial = (
        jnp.full((kv_here, per_kv, tokens_here), -1e30, jnp.float32),
        jnp.zeros((kv_here, per_kv, tokens_here), jnp.float32),
        jnp.zeros((kv_here, per_kv, tokens_here, DH), jnp.float32),
    )
    carry = initial
    key_piece = lax.all_gather(keys, "ctx", axis=0, tiled=True)
    value_piece = lax.all_gather(values, "ctx", axis=0, tiled=True)
    rows = key_piece.shape[0]
    width = 512
    number = rows // width
    key_blocks = key_piece.reshape(number, width, kv_here, DH)
    value_blocks = value_piece.reshape(number, width, kv_here, DH)

    def advance(inner, block_slice):
        key_block, value_block, index = block_slice
        block_start = index * width
        key_pos = block_start + jnp.arange(width, dtype=jnp.int32)
        inner = update(inner, key_block, value_block, key_pos)
        return (inner, None)

    carry, _ = lax.scan(
        advance, carry, (key_blocks, value_blocks, jnp.arange(number, dtype=jnp.int32))
    )
    peak, total_sum, summed = carry
    result = summed / total_sum[..., None]
    result = jnp.transpose(result, (2, 0, 1, 3)).reshape(tokens_here, kv_here * per_kv * DH)
    return result.astype(jnp.bfloat16)


def per_device(
    ssm_input,
    gate_input,
    in_state,
    out_state,
    step_size,
    log_decay,
    skip_gain,
    norm_gain,
    queries,
    keys,
    values,
):
    mamba_out = mamba_mixer(
        ssm_input, gate_input, in_state, out_state, step_size, log_decay, skip_gain, norm_gain
    )
    attention_out = attention(queries, keys, values)
    return (mamba_out, attention_out)


def solution(mesh):
    return jax.shard_map(
        per_device,
        mesh=mesh,
        in_specs=(
            P("ctx", "head"),
            P("ctx", "head"),
            P("ctx", "head"),
            P("ctx", "head"),
            P("ctx", "head"),
            P("ctx", "head"),
            P("head"),
            P("head"),
            P("ctx", "head"),
            P("ctx", "head"),
            P("ctx", "head"),
        ),
        out_specs=(P("ctx", "head"), P("ctx", "head")),
        check_vma=False,
    )
```

profile of v0, /device:TPU:231, one launch (start us, length us, event | category | flops | bytes accessed | tf_op | source)
XLA Modules:
  0.0 396.7 jit_solution(6865414195518606855)
XLA Ops:
  10.8 1.3 copy.67
  13.0 2.2 fusion.48
  15.9 28.9 %all_gather.16 = bf16[32,1,16]{2,1,0:T(2,128)(2,1)S(1)} all-gather(bf16[1,1,16]{2,1,0:T(2,128)(2,1)S(1)} %get-tuple-element.226), channel_id=1, replica_groups=mesh['ctx'=32,'head'=8] {'ctx'}, dimensions={0}, use_global_device_ids=true | all-gather | bytes 1056 | tf_op jit(solution)/shard_map/all_gather | solution.py:19
  45.3 1.3 copy.79
  46.8 6.7 %fusion.40 = f32[256,1,16,64]{0,3,2,1:T(8,128)} fusion(f32[256,256]{1,0:T(8,128)S(1)} %copy.73, f32[256,16]{0,1:T(8,128)S(1)} %copy.71, pred[256,256]{1,0:T(8,128)(4,1)} %iota_compare_fusion, f32[256,16,64]{0,2,1:T(8,128)S(1)} %bitcast.182, f32[256,16]{0,1:T(8,128)S(1)} %copy-done.3), kind=kOutput, calls=%fused_computation.47 | convolution fusion | flops 810811392 | bytes 2457600 | tf_op jit(solution)/shard_map/tsgk,sgkp->tgkp/dot_general | solution.py:47
  53.5 28.7 %all-gather.5.cloned.1.call-done = bf16[8192,128]{1,0:T(8,128)(2,1)} async-done(((bf16[256,128]{1,0:T(8,128)(2,1)}), bf16[8192,128]{1,0:T(8,128)(2,1)}) %all-gather.5.cloned.1.call-update) | async-done | bytes 2097168 | tf_op jit(solution)/shard_map/all_gather | solution.py:139
  82.3 77.7 %all-gather.7.cloned.1.call-done = bf16[8192,128]{1,0:T(8,128)(2,1)} async-done(((bf16[256,128]{1,0:T(8,128)(2,1)}), bf16[8192,128]{1,0:T(8,128)(2,1)}) %all-gather.7.cloned.1.call-update) | async-done | bytes 2097168 | tf_op jit(solution)/shard_map/all_gather | solution.py:140
  160.0 157.5 %while.28 = (s32[]{:T(128)}, f32[1,8,256]{2,1,0:T(8,128)S(1)}, f32[1,8,256]{2,1,0:T(8,128)S(1)}, f32[1,8,256,128]{3,2,1,0:T(8,128)S(1)}, s32[16]{0:T(128)S(1)}, ...) while((s32[]{:T(128)}, f32[1,8,256]{2,1,0:T(8,128)S(1)}, ...), condition=%wide.region_9.10_spmd.clone, body=%wide.region_6.9_spmd.clone.sunk | while | flops 549335808 | bytes 32906428 | solution.py:154
  161.4 3.7 fusion.72
  165.1 3.8 fusion.75
  171.2 3.7 fusion.72
  174.9 3.8 fusion.75
  181.1 3.7 fusion.72
  184.7 3.8 fusion.75
  190.9 3.7 fusion.72
  194.6 3.8 fusion.75
  200.8 3.7 fusion.72
  204.4 3.8 fusion.75
  210.6 3.7 fusion.72
  214.3 3.8 fusion.75
  220.4 3.7 fusion.72
  224.1 3.9 fusion.75
  230.3 3.7 fusion.72
  234.0 3.9 fusion.75
  240.3 3.7 fusion.72
  243.9 3.8 fusion.75
  250.1 3.7 fusion.72
  253.8 3.8 fusion.75
  260.0 3.7 fusion.72
  263.6 3.8 fusion.75
  269.8 3.7 fusion.72
  273.5 3.8 fusion.75
  279.6 3.7 fusion.72
  283.3 3.8 fusion.75
  289.4 3.7 fusion.72
  293.1 3.8 fusion.75
  299.3 3.7 fusion.72
  302.9 3.8 fusion.75
  309.1 3.7 fusion.72
  312.8 3.8 fusion.75
  319.2 48.5 %while.27 = (s32[]{:T(128)}, f32[1,16,128,64]{3,2,1,0:T(8,128)S(1)}, s32[]{:T(128)}, bf16[32,1,16]{2,1,0:T(2,128)(2,1)S(1)}, bf16[32,1,16,128,64]{3,4,2,0,1:T(8,128)(2,1)}, /*index=5*/s32[]{:T(128)}, s32[]{:T(128)}, s32[]{:T(128)}) while((s32[]{:T(128)}, f32[1,16,128,64]{3,2,1,0:T(8,128)S(1)}, s32[]{:T(128)}, ...), condition=%wide.region_3.4_spmd, body=%wide.region_2.3_spmd.sunk | while | flops 393237 | bytes 2359583 | solution.py:33
  319.2 1.0 constant_dynamic-slice_fusion.2
  320.8 1.0 constant_dynamic-slice_fusion.2
  322.4 1.0 constant_dynamic-slice_fusion.2
  323.9 1.0 constant_dynamic-slice_fusion.2
  325.5 1.0 constant_dynamic-slice_fusion.2
  327.0 1.0 constant_dynamic-slice_fusion.2
  328.6 1.0 constant_dynamic-slice_fusion.2
  330.2 1.0 constant_dynamic-slice_fusion.2
  333.3 1.0 constant_dynamic-slice_fusion.2
  334.9 1.0 constant_dynamic-slice_fusion.2
  336.4 1.0 constant_dynamic-slice_fusion.2
  338.0 1.0 constant_dynamic-slice_fusion.2
  341.1 1.0 constant_dynamic-slice_fusion.2
  342.7 1.0 constant_dynamic-slice_fusion.2
  344.2 1.0 constant_dynamic-slice_fusion.2
  345.8 1.0 constant_dynamic-slice_fusion.2
  348.9 1.0 constant_dynamic-slice_fusion.2
  350.5 1.0 constant_dynamic-slice_fusion.2
  352.1 1.0 constant_dynamic-slice_fusion.2
  367.7 2.3 fusion.45
  370.4 1.4 multiply_reduce_fusion
  371.8 16.2 %psum.7 = f32[256]{0:T(256)S(1)} all-reduce(f32[256]{0:T(256)S(1)} %multiply_reduce_fusion), channel_id=1, replica_groups=mesh['ctx'=32,'head'=8] {'head'}, use_global_device_ids=true, to_apply=%region_5.6 | all-reduce | flops 256 | bytes 2048 | tf_op jit(solution)/shard_map/psum | solution.py:99
  388.0 2.2 multiply_convert_fusion
  (313 shorter events, 62.9 us)
Async XLA Ops:
  7.2 37.7 %copy-start = (bf16[256,128]{1,0:T(8,128)(2,1)S(1)}, bf16[256,128]{1,0:T(8,128)(2,1)}, u32[]{:S(2)}) copy-start(bf16[256,128]{1,0:T(8,128)(2,1)} %param.18) | copy-start | bytes 196612
  7.2 37.7 %copy-start.2 = (bf16[256,128]{1,0:T(8,128)(2,1)S(1)}, bf16[256,128]{1,0:T(8,128)(2,1)}, u32[]{:S(2)}) copy-start(bf16[256,128]{1,0:T(8,128)(2,1)} %param.17) | copy-start | bytes 196612
  7.2 75.1 %all-gather.5.cloned.1.call-start = ((), (), s32[]{:S(2)}) async-start(), calls=%async_computation | async-start | bytes 2162688 | tf_op jit(solution)/shard_map/all_gather | solution.py:139
  7.9 152.1 %all-gather.7.cloned.1.call-start = ((), (), s32[]{:S(2)}) async-start(), calls=%async_computation.1 | async-start | bytes 2162688 | tf_op jit(solution)/shard_map/all_gather | solution.py:140
  8.7 310.4 %all-gather.9.cloned.1.call-start = ((), (), s32[]{:S(2)}) async-start(), calls=%async_computation.2 | async-start | bytes 8650752 | tf_op jit(solution)/shard_map/all_gather | solution.py:19
  12.1 34.8 %copy-start.3 = (f32[256,16]{0,1:T(8,128)S(1)}, f32[256,16]{0,1:T(8,128)}, u32[]{:S(2)}) copy-start(f32[256,16]{0,1:T(8,128)} %param.19) | copy-start | bytes 49156
  165.1 3.8 copy-start.1
  174.9 3.8 copy-start.1
  184.7 3.8 copy-start.1
  194.6 3.8 copy-start.1
  204.4 3.8 copy-start.1
  214.2 3.8 copy-start.1
  224.1 3.9 copy-start.1
  234.0 4.0 copy-start.1
  243.9 3.8 copy-start.1
  253.8 3.9 copy-start.1
  263.6 3.8 copy-start.1
  273.5 3.8 copy-start.1
  283.3 3.8 copy-start.1
  293.1 3.8 copy-start.1
  302.9 3.8 copy-start.1
  312.7 3.8 copy-start.1
  319.2 48.5 %copy-start.5 = (f32[16]{0:T(128)S(1)}, f32[16]{0:T(128)}, u32[]{:S(2)}) copy-start(f32[16]{0:T(128)} %param.21) | copy-start | bytes 196
  367.7 20.3 %copy-start.4 = (f32[1024]{0:T(1024)S(1)}, f32[1024]{0:T(1024)}, u32[]{:S(2)}) copy-start(f32[1024]{0:T(1024)} %param.22) | copy-start | bytes 12292
Sparse Core Ops, SparseCore 0:
  10.6 71.6 all-gather.4
  84.9 75.1 all-gather.6
  163.2 97.9 all-gather.8
where the time goes:
time: 399 us; the launch traced here: 397 us
  matrix products  131 us (33%)
  waiting for transfers between devices  108 us (27%)
  local copies, waits for them, and re-layouts  54.3 us (14%)
  blocking collectives  45.1 us (11%)
  other arithmetic  31.6 us (8%)
  between operations  13.9 us (3%)
  loops' own time  12.9 us (3%)
    all_gather x1, waiting for transfers between devices, attention(): value_piece = lax.all_gather(values, 'ctx', axis=0, tiled=True)  77.7 us
    dot_general x16, matrix products, update(): jnp.einsum('gqtj,jgd->gqtd', weight.astype(jnp.bfloat16), value_block, pr...  61 us
    dot_general x16, matrix products, update(): jnp.einsum('tgqd,jgd->gqtj', query_rows, key_block, preferred_element_typ...  58.5 us
    dynamic_slice x62, local copies, waits for them, and re-layouts, one(): lax.dynamic_index_in_dim(a, turn, 0, False).astype(own.dtype)  39 us
    all_gather x1, blocking collectives, carried_in(): lax.all_gather(a.astype(kind), axis)  28.9 us
    all_gather x1, waiting for transfers between devices, attention(): key_piece = lax.all_gather(keys, 'ctx', axis=0, tiled=True)  28.7 us
    psum x1, blocking collectives, mamba_mixer(): squares = lax.psum(jnp.sum(gated * gated, axis=1), 'head')  16.2 us
    reduce_sum x16, other arithmetic, update(): total_sum = total_sum * shrink + jnp.sum(weight, axis=-1)  14.1 us
  transfers between devices with their start and end apart: 3, of which 2 were waited for; matrix products, arithmetic and copies ran while one was open for 41% of the time, Pallas kernels for 0%

commit v1 on v0

--- a/solution.py
+++ b/solution.py
@@ -2,6 +2,7 @@
 import jax.numpy as jnp
 from jax import lax
 from jax.sharding import PartitionSpec as P
+from jax.lax import all_gather
 
 MIXER_HEADS = 128
 P_SIZE = 64
@@ -11,6 +12,12 @@
 DH = 128
 BLOCK = 256
 HIGH = lax.Precision.HIGHEST
+
+
+def trace_the_zone(inputs, field, a_name):
+    h_now = jnp.concatenate([field, inputs], axis=1)
+    then = all_gather(h_now, a_name, axis=0, tiled=True)
+    return jnp.split(then, [field.shape[1]], axis=1)
 
 
 def carried_in(value, axis, join, neutral):
@@ -136,8 +143,7 @@
         jnp.zeros((kv_here, per_kv, tokens_here, DH), jnp.float32),
     )
     carry = initial
-    key_piece = lax.all_gather(keys, "ctx", axis=0, tiled=True)
-    value_piece = lax.all_gather(values, "ctx", axis=0, tiled=True)
+    key_piece, value_piece = trace_the_zone(values, keys, "ctx")
     rows = key_piece.shape[0]
     width = 512
     number = rows // width

time: 399 us -> 330 us (0.83)
  waiting for transfers between devices: 108 us -> 35 us
  local copies, waits for them, and re-layouts: 54.3 us -> 58.7 us
    all_gather x2 -> x1, waiting for transfers between devices: 106 us -> 34.9 us  [trace_the_zone(): then = all_gather(h_now, a_name, axis=0, tiled=True)]
    split x0 -> x1, local copies, waits for them, and re-layouts: none -> 4.45 us  [trace_the_zone(): return jnp.split(then, [field.shape[1]], axis=1)]
  transfers between devices with their start and end apart: 3 -> 2, of which waited for: 2 -> 1; matrix products, arithmetic and copies ran while one was open for 41% -> 51% of each run, Pallas kernels for 0% -> 0%
where the time goes in v1:
time: 330 us; the launch traced here: 328 us
  matrix products  130 us (39%)
  local copies, waits for them, and re-layouts  58.7 us (18%)
  blocking collectives  44.5 us (13%)
  waiting for transfers between devices  35 us (11%)
  other arithmetic  32.9 us (10%)
  between operations  14.2 us (4%)
  loops' own time  13 us (4%)
    dot_general x16, matrix products, update(): jnp.einsum('gqtj,jgd->gqtd', weight.astype(jnp.bfloat16), value_block, pr...  60.9 us
    dot_general x16, matrix products, update(): jnp.einsum('tgqd,jgd->gqtj', query_rows, key_block, preferred_element_typ...  58.6 us
    dynamic_slice x62, local copies, waits for them, and re-layouts, one(): lax.dynamic_index_in_dim(a, turn, 0, False).astype(own.dtype)  39 us
    all_gather x1, waiting for transfers between devices, trace_the_zone(): then = all_gather(h_now, a_name, axis=0, tiled=True)  34.9 us
    all_gather x1, blocking collectives, carried_in(): lax.all_gather(a.astype(kind), axis)  28.4 us
    psum x1, blocking collectives, mamba_mixer(): squares = lax.psum(jnp.sum(gated * gated, axis=1), 'head')  16 us
    reduce_sum x16, other arithmetic, update(): total_sum = total_sum * shrink + jnp.sum(weight, axis=-1)  13.9 us
    another operation x1, loops' own time, attention(): lax.scan(advance, carry, (key_blocks, value_blocks, jnp.arange(number, dt...  11.6 us
  transfers between devices with their start and end apart: 2, of which 1 were waited for; matrix products, arithmetic and copies ran while one was open for 51% of the time, Pallas kernels for 0%

profile of v1, /device:TPU:231, one launch (start us, length us, event | category | flops | bytes accessed | tf_op | source)
XLA Modules:
  0.0 328.3 jit_solution(8471002405693364448)
XLA Ops:
  7.2 1.6 pad_maximum_fusion
  11.0 1.3 copy.67
  13.2 1.3 fusion.48
  15.2 28.4 %all_gather.13 = bf16[32,1,16]{2,1,0:T(2,128)(2,1)S(1)} all-gather(bf16[1,1,16]{2,1,0:T(2,128)(2,1)S(1)} %get-tuple-element.228), channel_id=1, replica_groups=mesh['ctx'=32,'head'=8] {'ctx'}, dimensions={0}, use_global_device_ids=true | all-gather | bytes 1056 | tf_op jit(solution)/shard_map/all_gather | solution.py:26
  44.1 1.3 copy.79
  45.7 6.7 %fusion.40 = f32[256,1,16,64]{0,3,2,1:T(8,128)} fusion(f32[256,256]{1,0:T(8,128)S(1)} %copy.73, f32[256,16]{0,1:T(8,128)S(1)} %copy.71, pred[256,256]{1,0:T(8,128)(4,1)} %iota_compare_fusion, f32[256,16,64]{0,2,1:T(8,128)S(1)} %bitcast.182, f32[256,16]{0,1:T(8,128)S(1)} %copy-done.3), kind=kOutput, calls=%fused_computation.47 | convolution fusion | flops 810811392 | bytes 2457600 | tf_op jit(solution)/shard_map/tsgk,sgkp->tgkp/dot_general | solution.py:54
  52.4 34.9 %all-gather.4.cloned.1.call-done = bf16[8192,256]{1,0:T(8,128)(2,1)} async-done(((bf16[256,256]{1,0:T(8,128)(2,1)}), bf16[8192,256]{1,0:T(8,128)(2,1)}) %all-gather.4.cloned.1.call-update) | async-done | bytes 4194320 | tf_op jit(solution)/shard_map/all_gather | solution.py:19
  87.3 4.5 %fusion.60 = (bf16[8192,128]{1,0:T(8,128)(2,1)}, bf16[8192,128]{1,0:T(8,128)(2,1)}) fusion(bf16[8192,256]{1,0:T(8,128)(2,1)} %all-gather.4.cloned.1.call-done), kind=kLoop, calls=%fused_computation.87 | loop fusion | bytes 8388608 | tf_op jit(solution)/shard_map/split | solution.py:20
  91.8 157.2 %while.28 = (s32[]{:T(128)}, f32[1,8,256]{2,1,0:T(8,128)S(1)}, f32[1,8,256]{2,1,0:T(8,128)S(1)}, f32[1,8,256,128]{3,2,1,0:T(8,128)S(1)}, s32[16]{0:T(128)S(1)}, ...) while((s32[]{:T(128)}, f32[1,8,256]{2,1,0:T(8,128)S(1)}, ...), condition=%wide.region_9.10_spmd.clone, body=%wide.region_6.9_spmd.clone.sunk | while | flops 549335808 | bytes 32906428 | solution.py:160
  93.2 3.7 %fusion.73 = (f32[8,256]{1,0:T(8,128)S(1)}, f32[512,256,8]{1,0,2:T(8,128)}) fusion(pred[256,512]{0,1:T(8,128)(4,1)S(1)} %broadcast_compare_fusion.2, bf16[256,1,8,128]{3,0,2,1:T(8,128)(2,1)S(1)} %get-tuple-element.378, bf16[16,512,1,128]{3,1,2,0:T(8,128)(2,1)} %get-tuple-element.377, s32[]{:T(128)} %get-tuple-element.360), kind=kOutput, calls=%fused_computation.6.clone.1 | convolution fusion | flops 271579136 | bytes 4989440 | tf_op jit(solution)/shard_map/while/body/eval_jaxpr/tgqd,jgd->gqtj/dot_general | solution.py:123
  96.8 3.8 %fusion.76 = f32[1,8,256,128]{3,2,1,0:T(8,128)S(1)} fusion(f32[512,256,8]{1,0,2:T(8,128)} %get-tuple-element.322, f32[8,256]{1,0:T(8,128)S(1)} %bitcast.187, pred[256,512]{0,1:T(8,128)(4,1)S(1)} %broadcast_compare_fusion.2, f32[1,8,256,128]{3,2,1,0:T(8,128)S(1)} %get-tuple-element.363, f32[8,256]{1,0:T(8,128)S(1)} %get-tuple-element.323, ...), kind=kOutput, calls=%fused_computation.15.clone.1 | convolution fusion | flops 273416192 | bytes 6570497 | tf_op jit(solution)/shard_map/while/body/eval_jaxpr/gqtj,jgd->gqtd/dot_general | solution.py:132
  103.0 3.7 %fusion.73 = (f32[8,256]{1,0:T(8,128)S(1)}, f32[512,256,8]{1,0,2:T(8,128)}) fusion(pred[256,512]{0,1:T(8,128)(4,1)S(1)} %broadcast_compare_fusion.2, bf16[256,1,8,128]{3,0,2,1:T(8,128)(2,1)S(1)} %get-tuple-element.378, bf16[16,512,1,128]{3,1,2,0:T(8,128)(2,1)} %get-tuple-element.377, s32[]{:T(128)} %get-tuple-element.360), kind=kOutput, calls=%fused_computation.6.clone.1 | convolution fusion | flops 271579136 | bytes 4989440 | tf_op jit(solution)/shard_map/while/body/eval_jaxpr/tgqd,jgd->gqtj/dot_general | solution.py:123
  106.6 3.9 %fusion.76 = f32[1,8,256,128]{3,2,1,0:T(8,128)S(1)} fusion(f32[512,256,8]{1,0,2:T(8,128)} %get-tuple-element.322, f32[8,256]{1,0:T(8,128)S(1)} %bitcast.187, pred[256,512]{0,1:T(8,128)(4,1)S(1)} %broadcast_compare_fusion.2, f32[1,8,256,128]{3,2,1,0:T(8,128)S(1)} %get-tuple-element.363, f32[8,256]{1,0:T(8,128)S(1)} %get-tuple-element.323, ...), kind=kOutput, calls=%fused_computation.15.clone.1 | convolution fusion | flops 273416192 | bytes 6570497 | tf_op jit(solution)/shard_map/while/body/eval_jaxpr/gqtj,jgd->gqtd/dot_general | solution.py:132
  112.9 3.7 %fusion.73 = (f32[8,256]{1,0:T(8,128)S(1)}, f32[512,256,8]{1,0,2:T(8,128)}) fusion(pred[256,512]{0,1:T(8,128)(4,1)S(1)} %broadcast_compare_fusion.2, bf16[256,1,8,128]{3,0,2,1:T(8,128)(2,1)S(1)} %get-tuple-element.378, bf16[16,512,1,128]{3,1,2,0:T(8,128)(2,1)} %get-tuple-element.377, s32[]{:T(128)} %get-tuple-element.360), kind=kOutput, calls=%fused_computation.6.clone.1 | convolution fusion | flops 271579136 | bytes 4989440 | tf_op jit(solution)/shard_map/while/body/eval_jaxpr/tgqd,jgd->gqtj/dot_general | solution.py:123
  116.5 3.8 %fusion.76 = f32[1,8,256,128]{3,2,1,0:T(8,128)S(1)} fusion(f32[512,256,8]{1,0,2:T(8,128)} %get-tuple-element.322, f32[8,256]{1,0:T(8,128)S(1)} %bitcast.187, pred[256,512]{0,1:T(8,128)(4,1)S(1)} %broadcast_compare_fusion.2, f32[1,8,256,128]{3,2,1,0:T(8,128)S(1)} %get-tuple-element.363, f32[8,256]{1,0:T(8,128)S(1)} %get-tuple-element.323, ...), kind=kOutput, calls=%fused_computation.15.clone.1 | convolution fusion | flops 273416192 | bytes 6570497 | tf_op jit(solution)/shard_map/while/body/eval_jaxpr/gqtj,jgd->gqtd/dot_general | solution.py:132
  122.7 3.7 %fusion.73 = (f32[8,256]{1,0:T(8,128)S(1)}, f32[512,256,8]{1,0,2:T(8,128)}) fusion(pred[256,512]{0,1:T(8,128)(4,1)S(1)} %broadcast_compare_fusion.2, bf16[256,1,8,128]{3,0,2,1:T(8,128)(2,1)S(1)} %get-tuple-element.378, bf16[16,512,1,128]{3,1,2,0:T(8,128)(2,1)} %get-tuple-element.377, s32[]{:T(128)} %get-tuple-element.360), kind=kOutput, calls=%fused_computation.6.clone.1 | convolution fusion | flops 271579136 | bytes 4989440 | tf_op jit(solution)/shard_map/while/body/eval_jaxpr/tgqd,jgd->gqtj/dot_general | solution.py:123
  126.4 3.8 %fusion.76 = f32[1,8,256,128]{3,2,1,0:T(8,128)S(1)} fusion(f32[512,256,8]{1,0,2:T(8,128)} %get-tuple-element.322, f32[8,256]{1,0:T(8,128)S(1)} %bitcast.187, pred[256,512]{0,1:T(8,128)(4,1)S(1)} %broadcast_compare_fusion.2, f32[1,8,256,128]{3,2,1,0:T(8,128)S(1)} %get-tuple-element.363, f32[8,256]{1,0:T(8,128)S(1)} %get-tuple-element.323, ...), kind=kOutput, calls=%fused_computation.15.clone.1 | convolution fusion | flops 273416192 | bytes 6570497 | tf_op jit(solution)/shard_map/while/body/eval_jaxpr/gqtj,jgd->gqtd/dot_general | solution.py:132
  132.5 3.7 %fusion.73 = (f32[8,256]{1,0:T(8,128)S(1)}, f32[512,256,8]{1,0,2:T(8,128)}) fusion(pred[256,512]{0,1:T(8,128)(4,1)S(1)} %broadcast_compare_fusion.2, bf16[256,1,8,128]{3,0,2,1:T(8,128)(2,1)S(1)} %get-tuple-element.378, bf16[16,512,1,128]{3,1,2,0:T(8,128)(2,1)} %get-tuple-element.377, s32[]{:T(128)} %get-tuple-element.360), kind=kOutput, calls=%fused_computation.6.clone.1 | convolution fusion | flops 271579136 | bytes 4989440 | tf_op jit(solution)/shard_map/while/body/eval_jaxpr/tgqd,jgd->gqtj/dot_general | solution.py:123
  136.2 3.8 %fusion.76 = f32[1,8,256,128]{3,2,1,0:T(8,128)S(1)} fusion(f32[512,256,8]{1,0,2:T(8,128)} %get-tuple-element.322, f32[8,256]{1,0:T(8,128)S(1)} %bitcast.187, pred[256,512]{0,1:T(8,128)(4,1)S(1)} %broadcast_compare_fusion.2, f32[1,8,256,128]{3,2,1,0:T(8,128)S(1)} %get-tuple-element.363, f32[8,256]{1,0:T(8,128)S(1)} %get-tuple-element.323, ...), kind=kOutput, calls=%fused_computation.15.clone.1 | convolution fusion | flops 273416192 | bytes 6570497 | tf_op jit(solution)/shard_map/while/body/eval_jaxpr/gqtj,jgd->gqtd/dot_general | solution.py:132
  142.3 3.7 %fusion.73 = (f32[8,256]{1,0:T(8,128)S(1)}, f32[512,256,8]{1,0,2:T(8,128)}) fusion(pred[256,512]{0,1:T(8,128)(4,1)S(1)} %broadcast_compare_fusion.2, bf16[256,1,8,128]{3,0,2,1:T(8,128)(2,1)S(1)} %get-tuple-element.378, bf16[16,512,1,128]{3,1,2,0:T(8,128)(2,1)} %get-tuple-element.377, s32[]{:T(128)} %get-tuple-element.360), kind=kOutput, calls=%fused_computation.6.clone.1 | convolution fusion | flops 271579136 | bytes 4989440 | tf_op jit(solution)/shard_map/while/body/eval_jaxpr/tgqd,jgd->gqtj/dot_general | solution.py:123
  146.0 3.8 %fusion.76 = f32[1,8,256,128]{3,2,1,0:T(8,128)S(1)} fusion(f32[512,256,8]{1,0,2:T(8,128)} %get-tuple-element.322, f32[8,256]{1,0:T(8,128)S(1)} %bitcast.187, pred[256,512]{0,1:T(8,128)(4,1)S(1)} %broadcast_compare_fusion.2, f32[1,8,256,128]{3,2,1,0:T(8,128)S(1)} %get-tuple-element.363, f32[8,256]{1,0:T(8,128)S(1)} %get-tuple-element.323, ...), kind=kOutput, calls=%fused_computation.15.clone.1 | convolution fusion | flops 273416192 | bytes 6570497 | tf_op jit(solution)/shard_map/while/body/eval_jaxpr/gqtj,jgd->gqtd/dot_general | solution.py:132
  152.1 3.7 %fusion.73 = (f32[8,256]{1,0:T(8,128)S(1)}, f32[512,256,8]{1,0,2:T(8,128)}) fusion(pred[256,512]{0,1:T(8,128)(4,1)S(1)} %broadcast_compare_fusion.2, bf16[256,1,8,128]{3,0,2,1:T(8,128)(2,1)S(1)} %get-tuple-element.378, bf16[16,512,1,128]{3,1,2,0:T(8,128)(2,1)} %get-tuple-element.377, s32[]{:T(128)} %get-tuple-element.360), kind=kOutput, calls=%fused_computation.6.clone.1 | convolution fusion | flops 271579136 | bytes 4989440 | tf_op jit(solution)/shard_map/while/body/eval_jaxpr/tgqd,jgd->gqtj/dot_general | solution.py:123
  155.8 3.8 %fusion.76 = f32[1,8,256,128]{3,2,1,0:T(8,128)S(1)} fusion(f32[512,256,8]{1,0,2:T(8,128)} %get-tuple-element.322, f32[8,256]{1,0:T(8,128)S(1)} %bitcast.187, pred[256,512]{0,1:T(8,128)(4,1)S(1)} %broadcast_compare_fusion.2, f32[1,8,256,128]{3,2,1,0:T(8,128)S(1)} %get-tuple-element.363, f32[8,256]{1,0:T(8,128)S(1)} %get-tuple-element.323, ...), kind=kOutput, calls=%fused_computation.15.clone.1 | convolution fusion | flops 273416192 | bytes 6570497 | tf_op jit(solution)/shard_map/while/body/eval_jaxpr/gqtj,jgd->gqtd/dot_general | solution.py:132
  161.9 3.7 %fusion.73 = (f32[8,256]{1,0:T(8,128)S(1)}, f32[512,256,8]{1,0,2:T(8,128)}) fusion(pred[256,512]{0,1:T(8,128)(4,1)S(1)} %broadcast_compare_fusion.2, bf16[256,1,8,128]{3,0,2,1:T(8,128)(2,1)S(1)} %get-tuple-element.378, bf16[16,512,1,128]{3,1,2,0:T(8,128)(2,1)} %get-tuple-element.377, s32[]{:T(128)} %get-tuple-element.360), kind=kOutput, calls=%fused_computation.6.clone.1 | convolution fusion | flops 271579136 | bytes 4989440 | tf_op jit(solution)/shard_map/while/body/eval_jaxpr/tgqd,jgd->gqtj/dot_general | solution.py:123
  165.6 3.9 %fusion.76 = f32[1,8,256,128]{3,2,1,0:T(8,128)S(1)} fusion(f32[512,256,8]{1,0,2:T(8,128)} %get-tuple-element.322, f32[8,256]{1,0:T(8,128)S(1)} %bitcast.187, pred[256,512]{0,1:T(8,128)(4,1)S(1)} %broadcast_compare_fusion.2, f32[1,8,256,128]{3,2,1,0:T(8,128)S(1)} %get-tuple-element.363, f32[8,256]{1,0:T(8,128)S(1)} %get-tuple-element.323, ...), kind=kOutput, calls=%fused_computation.15.clone.1 | convolution fusion | flops 273416192 | bytes 6570497 | tf_op jit(solution)/shard_map/while/body/eval_jaxpr/gqtj,jgd->gqtd/dot_general | solution.py:132
  171.9 3.7 %fusion.73 = (f32[8,256]{1,0:T(8,128)S(1)}, f32[512,256,8]{1,0,2:T(8,128)}) fusion(pred[256,512]{0,1:T(8,128)(4,1)S(1)} %broadcast_compare_fusion.2, bf16[256,1,8,128]{3,0,2,1:T(8,128)(2,1)S(1)} %get-tuple-element.378, bf16[16,512,1,128]{3,1,2,0:T(8,128)(2,1)} %get-tuple-element.377, s32[]{:T(128)} %get-tuple-element.360), kind=kOutput, calls=%fused_computation.6.clone.1 | convolution fusion | flops 271579136 | bytes 4989440 | tf_op jit(solution)/shard_map/while/body/eval_jaxpr/tgqd,jgd->gqtj/dot_general | solution.py:123
  175.5 3.8 %fusion.76 = f32[1,8,256,128]{3,2,1,0:T(8,128)S(1)} fusion(f32[512,256,8]{1,0,2:T(8,128)} %get-tuple-element.322, f32[8,256]{1,0:T(8,128)S(1)} %bitcast.187, pred[256,512]{0,1:T(8,128)(4,1)S(1)} %broadcast_compare_fusion.2, f32[1,8,256,128]{3,2,1,0:T(8,128)S(1)} %get-tuple-element.363, f32[8,256]{1,0:T(8,128)S(1)} %get-tuple-element.323, ...), kind=kOutput, calls=%fused_computation.15.clone.1 | convolution fusion | flops 273416192 | bytes 6570497 | tf_op jit(solution)/shard_map/while/body/eval_jaxpr/gqtj,jgd->gqtd/dot_general | solution.py:132
  181.7 3.7 %fusion.73 = (f32[8,256]{1,0:T(8,128)S(1)}, f32[512,256,8]{1,0,2:T(8,128)}) fusion(pred[256,512]{0,1:T(8,128)(4,1)S(1)} %broadcast_compare_fusion.2, bf16[256,1,8,128]{3,0,2,1:T(8,128)(2,1)S(1)} %get-tuple-element.378, bf16[16,512,1,128]{3,1,2,0:T(8,128)(2,1)} %get-tuple-element.377, s32[]{:T(128)} %get-tuple-element.360), kind=kOutput, calls=%fused_computation.6.clone.1 | convolution fusion | flops 271579136 | bytes 4989440 | tf_op jit(solution)/shard_map/while/body/eval_jaxpr/tgqd,jgd->gqtj/dot_general | solution.py:123
  185.3 3.8 %fusion.76 = f32[1,8,256,128]{3,2,1,0:T(8,128)S(1)} fusion(f32[512,256,8]{1,0,2:T(8,128)} %get-tuple-element.322, f32[8,256]{1,0:T(8,128)S(1)} %bitcast.187, pred[256,512]{0,1:T(8,128)(4,1)S(1)} %broadcast_compare_fusion.2, f32[1,8,256,128]{3,2,1,0:T(8,128)S(1)} %get-tuple-element.363, f32[8,256]{1,0:T(8,128)S(1)} %get-tuple-element.323, ...), kind=kOutput, calls=%fused_computation.15.clone.1 | convolution fusion | flops 273416192 | bytes 6570497 | tf_op jit(solution)/shard_map/while/body/eval_jaxpr/gqtj,jgd->gqtd/dot_general | solution.py:132
  191.5 3.7 %fusion.73 = (f32[8,256]{1,0:T(8,128)S(1)}, f32[512,256,8]{1,0,2:T(8,128)}) fusion(pred[256,512]{0,1:T(8,128)(4,1)S(1)} %broadcast_compare_fusion.2, bf16[256,1,8,128]{3,0,2,1:T(8,128)(2,1)S(1)} %get-tuple-element.378, bf16[16,512,1,128]{3,1,2,0:T(8,128)(2,1)} %get-tuple-element.377, s32[]{:T(128)} %get-tuple-element.360), kind=kOutput, calls=%fused_computation.6.clone.1 | convolution fusion | flops 271579136 | bytes 4989440 | tf_op jit(solution)/shard_map/while/body/eval_jaxpr/tgqd,jgd->gqtj/dot_general | solution.py:123
  195.2 3.8 %fusion.76 = f32[1,8,256,128]{3,2,1,0:T(8,128)S(1)} fusion(f32[512,256,8]{1,0,2:T(8,128)} %get-tuple-element.322, f32[8,256]{1,0:T(8,128)S(1)} %bitcast.187, pred[256,512]{0,1:T(8,128)(4,1)S(1)} %broadcast_compare_fusion.2, f32[1,8,256,128]{3,2,1,0:T(8,128)S(1)} %get-tuple-element.363, f32[8,256]{1,0:T(8,128)S(1)} %get-tuple-element.323, ...), kind=kOutput, calls=%fused_computation.15.clone.1 | convolution fusion | flops 273416192 | bytes 6570497 | tf_op jit(solution)/shard_map/while/body/eval_jaxpr/gqtj,jgd->gqtd/dot_general | solution.py:132
  201.3 3.7 %fusion.73 = (f32[8,256]{1,0:T(8,128)S(1)}, f32[512,256,8]{1,0,2:T(8,128)}) fusion(pred[256,512]{0,1:T(8,128)(4,1)S(1)} %broadcast_compare_fusion.2, bf16[256,1,8,128]{3,0,2,1:T(8,128)(2,1)S(1)} %get-tuple-element.378, bf16[16,512,1,128]{3,1,2,0:T(8,128)(2,1)} %get-tuple-element.377, s32[]{:T(128)} %get-tuple-element.360), kind=kOutput, calls=%fused_computation.6.clone.1 | convolution fusion | flops 271579136 | bytes 4989440 | tf_op jit(solution)/shard_map/while/body/eval_jaxpr/tgqd,jgd->gqtj/dot_general | solution.py:123
  205.0 3.8 %fusion.76 = f32[1,8,256,128]{3,2,1,0:T(8,128)S(1)} fusion(f32[512,256,8]{1,0,2:T(8,128)} %get-tuple-element.322, f32[8,256]{1,0:T(8,128)S(1)} %bitcast.187, pred[256,512]{0,1:T(8,128)(4,1)S(1)} %broadcast_compare_fusion.2, f32[1,8,256,128]{3,2,1,0:T(8,128)S(1)} %get-tuple-element.363, f32[8,256]{1,0:T(8,128)S(1)} %get-tuple-element.323, ...), kind=kOutput, calls=%fused_computation.15.clone.1 | convolution fusion | flops 273416192 | bytes 6570497 | tf_op jit(solution)/shard_map/while/body/eval_jaxpr/gqtj,jgd->gqtd/dot_general | solution.py:132
  211.1 3.7 %fusion.73 = (f32[8,256]{1,0:T(8,128)S(1)}, f32[512,256,8]{1,0,2:T(8,128)}) fusion(pred[256,512]{0,1:T(8,128)(4,1)S(1)} %broadcast_compare_fusion.2, bf16[256,1,8,128]{3,0,2,1:T(8,128)(2,1)S(1)} %get-tuple-element.378, bf16[16,512,1,128]{3,1,2,0:T(8,128)(2,1)} %get-tuple-element.377, s32[]{:T(128)} %get-tuple-element.360), kind=kOutput, calls=%fused_computation.6.clone.1 | convolution fusion | flops 271579136 | bytes 4989440 | tf_op jit(solution)/shard_map/while/body/eval_jaxpr/tgqd,jgd->gqtj/dot_general | solution.py:123
  214.8 3.8 %fusion.76 = f32[1,8,256,128]{3,2,1,0:T(8,128)S(1)} fusion(f32[512,256,8]{1,0,2:T(8,128)} %get-tuple-element.322, f32[8,256]{1,0:T(8,128)S(1)} %bitcast.187, pred[256,512]{0,1:T(8,128)(4,1)S(1)} %broadcast_compare_fusion.2, f32[1,8,256,128]{3,2,1,0:T(8,128)S(1)} %get-tuple-element.363, f32[8,256]{1,0:T(8,128)S(1)} %get-tuple-element.323, ...), kind=kOutput, calls=%fused_computation.15.clone.1 | convolution fusion | flops 273416192 | bytes 6570497 | tf_op jit(solution)/shard_map/while/body/eval_jaxpr/gqtj,jgd->gqtd/dot_general | solution.py:132
  220.9 3.7 %fusion.73 = (f32[8,256]{1,0:T(8,128)S(1)}, f32[512,256,8]{1,0,2:T(8,128)}) fusion(pred[256,512]{0,1:T(8,128)(4,1)S(1)} %broadcast_compare_fusion.2, bf16[256,1,8,128]{3,0,2,1:T(8,128)(2,1)S(1)} %get-tuple-element.378, bf16[16,512,1,128]{3,1,2,0:T(8,128)(2,1)} %get-tuple-element.377, s32[]{:T(128)} %get-tuple-element.360), kind=kOutput, calls=%fused_computation.6.clone.1 | convolution fusion | flops 271579136 | bytes 4989440 | tf_op jit(solution)/shard_map/while/body/eval_jaxpr/tgqd,jgd->gqtj/dot_general | solution.py:123
  224.6 3.8 %fusion.76 = f32[1,8,256,128]{3,2,1,0:T(8,128)S(1)} fusion(f32[512,256,8]{1,0,2:T(8,128)} %get-tuple-element.322, f32[8,256]{1,0:T(8,128)S(1)} %bitcast.187, pred[256,512]{0,1:T(8,128)(4,1)S(1)} %broadcast_compare_fusion.2, f32[1,8,256,128]{3,2,1,0:T(8,128)S(1)} %get-tuple-element.363, f32[8,256]{1,0:T(8,128)S(1)} %get-tuple-element.323, ...), kind=kOutput, calls=%fused_computation.15.clone.1 | convolution fusion | flops 273416192 | bytes 6570497 | tf_op jit(solution)/shard_map/while/body/eval_jaxpr/gqtj,jgd->gqtd/dot_general | solution.py:132
  230.7 3.7 %fusion.73 = (f32[8,256]{1,0:T(8,128)S(1)}, f32[512,256,8]{1,0,2:T(8,128)}) fusion(pred[256,512]{0,1:T(8,128)(4,1)S(1)} %broadcast_compare_fusion.2, bf16[256,1,8,128]{3,0,2,1:T(8,128)(2,1)S(1)} %get-tuple-element.378, bf16[16,512,1,128]{3,1,2,0:T(8,128)(2,1)} %get-tuple-element.377, s32[]{:T(128)} %get-tuple-element.360), kind=kOutput, calls=%fused_computation.6.clone.1 | convolution fusion | flops 271579136 | bytes 4989440 | tf_op jit(solution)/shard_map/while/body/eval_jaxpr/tgqd,jgd->gqtj/dot_general | solution.py:123
  234.4 3.8 %fusion.76 = f32[1,8,256,128]{3,2,1,0:T(8,128)S(1)} fusion(f32[512,256,8]{1,0,2:T(8,128)} %get-tuple-element.322, f32[8,256]{1,0:T(8,128)S(1)} %bitcast.187, pred[256,512]{0,1:T(8,128)(4,1)S(1)} %broadcast_compare_fusion.2, f32[1,8,256,128]{3,2,1,0:T(8,128)S(1)} %get-tuple-element.363, f32[8,256]{1,0:T(8,128)S(1)} %get-tuple-element.323, ...), kind=kOutput, calls=%fused_computation.15.clone.1 | convolution fusion | flops 273416192 | bytes 6570497 | tf_op jit(solution)/shard_map/while/body/eval_jaxpr/gqtj,jgd->gqtd/dot_general | solution.py:132
  240.5 3.7 %fusion.73 = (f32[8,256]{1,0:T(8,128)S(1)}, f32[512,256,8]{1,0,2:T(8,128)}) fusion(pred[256,512]{0,1:T(8,128)(4,1)S(1)} %broadcast_compare_fusion.2, bf16[256,1,8,128]{3,0,2,1:T(8,128)(2,1)S(1)} %get-tuple-element.378, bf16[16,512,1,128]{3,1,2,0:T(8,128)(2,1)} %get-tuple-element.377, s32[]{:T(128)} %get-tuple-element.360), kind=kOutput, calls=%fused_computation.6.clone.1 | convolution fusion | flops 271579136 | bytes 4989440 | tf_op jit(solution)/shard_map/while/body/eval_jaxpr/tgqd,jgd->gqtj/dot_general | solution.py:123
  244.2 3.8 %fusion.76 = f32[1,8,256,128]{3,2,1,0:T(8,128)S(1)} fusion(f32[512,256,8]{1,0,2:T(8,128)} %get-tuple-element.322, f32[8,256]{1,0:T(8,128)S(1)} %bitcast.187, pred[256,512]{0,1:T(8,128)(4,1)S(1)} %broadcast_compare_fusion.2, f32[1,8,256,128]{3,2,1,0:T(8,128)S(1)} %get-tuple-element.363, f32[8,256]{1,0:T(8,128)S(1)} %get-tuple-element.323, ...), kind=kOutput, calls=%fused_computation.15.clone.1 | convolution fusion | flops 273416192 | bytes 6570497 | tf_op jit(solution)/shard_map/while/body/eval_jaxpr/gqtj,jgd->gqtd/dot_general | solution.py:132
  250.6 48.5 %while.27 = (s32[]{:T(128)}, f32[1,16,128,64]{3,2,1,0:T(8,128)S(1)}, s32[]{:T(128)}, bf16[32,1,16]{2,1,0:T(2,128)(2,1)S(1)}, bf16[32,1,16,128,64]{3,4,2,0,1:T(8,128)(2,1)}, /*index=5*/s32[]{:T(128)}, s32[]{:T(128)}, s32[]{:T(128)}) while((s32[]{:T(128)}, f32[1,16,128,64]{3,2,1,0:T(8,128)S(1)}, s32[]{:T(128)}, ...), condition=%wide.region_3.4_spmd, body=%wide.region_2.3_spmd.sunk | while | flops 393237 | bytes 2359583 | solution.py:40
  250.7 1.0 constant_dynamic-slice_fusion.2
  253.8 1.0 constant_dynamic-slice_fusion.2
  255.4 1.0 constant_dynamic-slice_fusion.2
  256.9 1.0 constant_dynamic-slice_fusion.2
  258.5 1.0 constant_dynamic-slice_fusion.2
  261.6 1.0 constant_dynamic-slice_fusion.2
  263.2 1.0 constant_dynamic-slice_fusion.2
  264.7 1.0 constant_dynamic-slice_fusion.2
  266.3 1.0 constant_dynamic-slice_fusion.2
  269.4 1.0 constant_dynamic-slice_fusion.2
  271.0 1.0 constant_dynamic-slice_fusion.2
  272.6 1.0 constant_dynamic-slice_fusion.2
  274.1 1.0 constant_dynamic-slice_fusion.2
  275.7 1.0 constant_dynamic-slice_fusion.2
  277.2 1.0 constant_dynamic-slice_fusion.2
  278.8 1.0 constant_dynamic-slice_fusion.2
  280.4 1.0 constant_dynamic-slice_fusion.2
  283.5 1.0 constant_dynamic-slice_fusion.2
  299.1 2.3 fusion.45
  301.8 1.4 multiply_reduce_fusion
  303.3 16.0 %psum.7 = f32[256]{0:T(256)S(1)} all-reduce(f32[256]{0:T(256)S(1)} %multiply_reduce_fusion), channel_id=1, replica_groups=mesh['ctx'=32,'head'=8] {'head'}, use_global_device_ids=true, to_apply=%region_5.6 | all-reduce | flops 256 | bytes 2048 | tf_op jit(solution)/shard_map/psum | solution.py:106
  319.3 2.2 multiply_convert_fusion
  (312 shorter events, 62.2 us)
Async XLA Ops:
  7.2 36.6 %copy-start = (bf16[256,128]{1,0:T(8,128)(2,1)S(1)}, bf16[256,128]{1,0:T(8,128)(2,1)}, u32[]{:S(2)}) copy-start(bf16[256,128]{1,0:T(8,128)(2,1)} %param.18) | copy-start | bytes 196612
  7.2 6.0 %copy-start.2 = (bf16[256,128]{1,0:T(8,128)(2,1)S(1)}, bf16[256,128]{1,0:T(8,128)(2,1)}, u32[]{:S(2)}) copy-start(bf16[256,128]{1,0:T(8,128)(2,1)} %param.17) | copy-start | bytes 196612
  7.2 80.1 %all-gather.4.cloned.1.call-start = ((), (), s32[]{:S(2)}) async-start(), calls=%async_computation | async-start | bytes 4325376 | tf_op jit(solution)/shard_map/all_gather | solution.py:19
  8.8 241.7 %all-gather.6.cloned.1.call-start = ((), (), s32[]{:S(2)}) async-start(), calls=%async_computation.1 | async-start | bytes 8650752 | tf_op jit(solution)/shard_map/all_gather | solution.py:26
  12.2 33.4 %copy-start.3 = (f32[256,16]{0,1:T(8,128)S(1)}, f32[256,16]{0,1:T(8,128)}, u32[]{:S(2)}) copy-start(f32[256,16]{0,1:T(8,128)} %param.19) | copy-start | bytes 49156
  96.8 3.8 %copy-start.1 = (f32[512,256,8]{1,0,2:T(8,128)S(1)}, f32[512,256,8]{1,0,2:T(8,128)}, u32[]{:S(2)}) copy-start(f32[512,256,8]{1,0,2:T(8,128)} %get-tuple-element.322) | copy-start | bytes 12582916 | tf_op jit(solution)/shard_map/while
  106.6 3.9 %copy-start.1 = (f32[512,256,8]{1,0,2:T(8,128)S(1)}, f32[512,256,8]{1,0,2:T(8,128)}, u32[]{:S(2)}) copy-start(f32[512,256,8]{1,0,2:T(8,128)} %get-tuple-element.322) | copy-start | bytes 12582916 | tf_op jit(solution)/shard_map/while
  116.5 3.8 %copy-start.1 = (f32[512,256,8]{1,0,2:T(8,128)S(1)}, f32[512,256,8]{1,0,2:T(8,128)}, u32[]{:S(2)}) copy-start(f32[512,256,8]{1,0,2:T(8,128)} %get-tuple-element.322) | copy-start | bytes 12582916 | tf_op jit(solution)/shard_map/while
  126.3 3.8 %copy-start.1 = (f32[512,256,8]{1,0,2:T(8,128)S(1)}, f32[512,256,8]{1,0,2:T(8,128)}, u32[]{:S(2)}) copy-start(f32[512,256,8]{1,0,2:T(8,128)} %get-tuple-element.322) | copy-start | bytes 12582916 | tf_op jit(solution)/shard_map/while
  136.1 3.8 %copy-start.1 = (f32[512,256,8]{1,0,2:T(8,128)S(1)}, f32[512,256,8]{1,0,2:T(8,128)}, u32[]{:S(2)}) copy-start(f32[512,256,8]{1,0,2:T(8,128)} %get-tuple-element.322) | copy-start | bytes 12582916 | tf_op jit(solution)/shard_map/while
  146.0 3.8 %copy-start.1 = (f32[512,256,8]{1,0,2:T(8,128)S(1)}, f32[512,256,8]{1,0,2:T(8,128)}, u32[]{:S(2)}) copy-start(f32[512,256,8]{1,0,2:T(8,128)} %get-tuple-element.322) | copy-start | bytes 12582916 | tf_op jit(solution)/shard_map/while
  155.8 3.8 %copy-start.1 = (f32[512,256,8]{1,0,2:T(8,128)S(1)}, f32[512,256,8]{1,0,2:T(8,128)}, u32[]{:S(2)}) copy-start(f32[512,256,8]{1,0,2:T(8,128)} %get-tuple-element.322) | copy-start | bytes 12582916 | tf_op jit(solution)/shard_map/while
  165.6 3.9 %copy-start.1 = (f32[512,256,8]{1,0,2:T(8,128)S(1)}, f32[512,256,8]{1,0,2:T(8,128)}, u32[]{:S(2)}) copy-start(f32[512,256,8]{1,0,2:T(8,128)} %get-tuple-element.322) | copy-start | bytes 12582916 | tf_op jit(solution)/shard_map/while
  175.5 3.8 %copy-start.1 = (f32[512,256,8]{1,0,2:T(8,128)S(1)}, f32[512,256,8]{1,0,2:T(8,128)}, u32[]{:S(2)}) copy-start(f32[512,256,8]{1,0,2:T(8,128)} %get-tuple-element.322) | copy-start | bytes 12582916 | tf_op jit(solution)/shard_map/while
  185.3 3.8 %copy-start.1 = (f32[512,256,8]{1,0,2:T(8,128)S(1)}, f32[512,256,8]{1,0,2:T(8,128)}, u32[]{:S(2)}) copy-start(f32[512,256,8]{1,0,2:T(8,128)} %get-tuple-element.322) | copy-start | bytes 12582916 | tf_op jit(solution)/shard_map/while
  195.1 3.8 %copy-start.1 = (f32[512,256,8]{1,0,2:T(8,128)S(1)}, f32[512,256,8]{1,0,2:T(8,128)}, u32[]{:S(2)}) copy-start(f32[512,256,8]{1,0,2:T(8,128)} %get-tuple-element.322) | copy-start | bytes 12582916 | tf_op jit(solution)/shard_map/while
  205.0 3.8 %copy-start.1 = (f32[512,256,8]{1,0,2:T(8,128)S(1)}, f32[512,256,8]{1,0,2:T(8,128)}, u32[]{:S(2)}) copy-start(f32[512,256,8]{1,0,2:T(8,128)} %get-tuple-element.322) | copy-start | bytes 12582916 | tf_op jit(solution)/shard_map/while
  214.8 3.8 %copy-start.1 = (f32[512,256,8]{1,0,2:T(8,128)S(1)}, f32[512,256,8]{1,0,2:T(8,128)}, u32[]{:S(2)}) copy-start(f32[512,256,8]{1,0,2:T(8,128)} %get-tuple-element.322) | copy-start | bytes 12582916 | tf_op jit(solution)/shard_map/while
  224.6 3.8 %copy-start.1 = (f32[512,256,8]{1,0,2:T(8,128)S(1)}, f32[512,256,8]{1,0,2:T(8,128)}, u32[]{:S(2)}) copy-start(f32[512,256,8]{1,0,2:T(8,128)} %get-tuple-element.322) | copy-start | bytes 12582916 | tf_op jit(solution)/shard_map/while
  234.4 3.8 %copy-start.1 = (f32[512,256,8]{1,0,2:T(8,128)S(1)}, f32[512,256,8]{1,0,2:T(8,128)}, u32[]{:S(2)}) copy-start(f32[512,256,8]{1,0,2:T(8,128)} %get-tuple-element.322) | copy-start | bytes 12582916 | tf_op jit(solution)/shard_map/while
  244.2 3.8 %copy-start.1 = (f32[512,256,8]{1,0,2:T(8,128)S(1)}, f32[512,256,8]{1,0,2:T(8,128)}, u32[]{:S(2)}) copy-start(f32[512,256,8]{1,0,2:T(8,128)} %get-tuple-element.322) | copy-start | bytes 12582916 | tf_op jit(solution)/shard_map/while
  250.6 48.5 %copy-start.5 = (f32[16]{0:T(128)S(1)}, f32[16]{0:T(128)}, u32[]{:S(2)}) copy-start(f32[16]{0:T(128)} %param.21) | copy-start | bytes 196
  299.1 20.2 %copy-start.4 = (f32[1024]{0:T(1024)S(1)}, f32[1024]{0:T(1024)}, u32[]{:S(2)}) copy-start(f32[1024]{0:T(1024)} %param.22) | copy-start | bytes 12292
Sparse Core Ops, SparseCore 0:
  11.2 76.0 all-gather.3
  90.5 97.4 all-gather.5
